TPU v7x, 32 devices: a whole 2x2x4 slice. The times are simulated.
32 devices in a mesh: grp: 8 (over y, x, core), tp: 4 (over z).
Axes of the slice: x: 2, y: 2, z: 4, core: 2. Of those that a mesh axis runs over, the one named last changes fastest.
Arguments:
- queries: bfloat16 [16, 64, 256, 128], P('grp', 'tp'), may hold values from -8 to 8
- new_kv: bfloat16 [16, 8, 256, 256], P('grp', 'tp'), may hold values from -4.5 to 4.5
- kv_pool: bfloat16 [1024, 8, 128, 256], P(('grp', 'tp')), may hold values from -4.5 to 4.5
- cache_lens: int32 [16], replicated, may hold values from 1 to 7936, 63488 in all
- session_seat: int32 [16], replicated, may hold values from 0 to 15, as said below
- old_slots: int32 [16, 64], replicated, may hold values from 0 to 1023, as said below
- new_slots: int32 [16, 64], replicated, may hold values from 0 to 1023, as said below
Outputs:
- attention: bfloat16 [16, 64, 256, 128], P('grp', 'tp')
- new_pool: bfloat16 [1024, 8, 128, 256], P(('grp', 'tp'))
Inputs may be any that keep to these rules, and one draw needn't show every extreme that they name: `session_seat`: A permutation of the sessions. `old_slots`: every pool block appears exactly once. Call the group of session s session_seat[s] // 2; every device of grp+tp holds exactly 4 of its 32 blocks for the sessions of each group. `new_slots`: every pool block appears exactly once, and every device holds exactly 4 blocks for the sessions of each group, as for old_slots.
All inputs are finite; a program needn't handle non-finite values.
Results may differ from a plain program's by a relative error of at most 0.005.
Values may be sent and summed in bfloat16 or wider, within the bound.
A program may use at most 128 MiB of HBM per device.

v0:
```python
import jax
import jax.numpy as jnp
from jax import lax
from jax.sharding import PartitionSpec as P


def slot_layout(slot_map, owners, pool_dev, seats_group, max_blocks):
    slot_count = owners * pool_dev
    seat_count = slot_map.shape[0]
    labels = (
        jnp.arange(seat_count, dtype=jnp.int32)[:, None] * max_blocks
        + jnp.arange(max_blocks, dtype=jnp.int32)[None, :]
    )
    content = (
        jnp.zeros((slot_count,), jnp.int32)
        .at[slot_map.reshape(-1)]
        .set(labels.reshape(-1))
        .reshape(owners, pool_dev)
    )
    holder = content // (max_blocks * seats_group)
    local_ids = jnp.arange(pool_dev, dtype=jnp.int32)
    earlier = local_ids[None, :] < local_ids[:, None]
    same_group = holder[:, :, None] == holder[:, None, :]
    ranking = jnp.sum(jnp.logical_and(same_group, earlier[None]), axis=2)
    return (content, holder, ranking)


def attend_block(query_rows, limits, key_rows, value_rows):
    head_dim = query_rows.shape[1]
    scores = lax.dot_general(
        query_rows, key_rows, (((1,), (1,)), ((), ())), preferred_element_type=jnp.float32
    ) * head_dim ** (-0.5)
    column = jnp.arange(key_rows.shape[0], dtype=jnp.int32)
    scores = jnp.where(column[None, :] <= limits[:, None], scores, -1e30)
    highest = jnp.max(scores, axis=1, keepdims=True)
    weights = jnp.exp(scores - highest)
    weights = (weights / jnp.sum(weights, axis=1, keepdims=True)).astype(jnp.bfloat16)
    return jnp.dot(weights, value_rows, preferred_element_type=jnp.float32).astype(jnp.bfloat16)


def local(queries, new_kv, kv_pool, cache_lens, session_seat, old_slots, new_slots):
    group_count = lax.axis_size("grp")
    tp_count = lax.axis_size("tp")
    owners = group_count * tp_count
    pool_dev, kv_heads, block_len, pair_width = kv_pool.shape
    head_dim = pair_width // 2
    seats_group, qh_dev, turn, unused_dim = queries.shape
    kvh_dev = new_kv.shape[1]
    seat_count = session_seat.shape[0]
    max_blocks = old_slots.shape[1]
    group_share = pool_dev // group_count
    key_span = max_blocks * block_len
    group_index = lax.axis_index("grp")
    tp_index = lax.axis_index("tp")
    my_index = group_index * tp_count + tp_index
    seat_session = (
        jnp.zeros((seat_count,), jnp.int32)
        .at[session_seat]
        .set(jnp.arange(seat_count, dtype=jnp.int32))
    )
    seat_lens = cache_lens[seat_session]
    old_table = old_slots[seat_session]
    new_table = new_slots[seat_session]
    my_lens = lax.dynamic_slice_in_dim(seat_lens, group_index * seats_group, seats_group, 0)
    old_content, old_holder, old_rank = slot_layout(
        old_table, owners, pool_dev, seats_group, max_blocks
    )
    my_holder = lax.dynamic_index_in_dim(old_holder, my_index, 0, keepdims=False)
    my_rank = lax.dynamic_index_in_dim(old_rank, my_index, 0, keepdims=False)
    send_order = (
        jnp.zeros((pool_dev,), jnp.int32)
        .at[my_holder * group_share + my_rank]
        .set(jnp.arange(pool_dev, dtype=jnp.int32))
    )
    target_ids = jnp.arange(owners, dtype=jnp.int32)
    target_group = target_ids // tp_count
    target_tp = target_ids % tp_count
    slot_pick = send_order[
        target_group[:, None] * group_share + jnp.arange(group_share, dtype=jnp.int32)[None, :]
    ]
    head_pick = (
        target_tp[:, None, None] * kvh_dev + jnp.arange(kvh_dev, dtype=jnp.int32)[None, None, :]
    )
    row_index = slot_pick[:, :, None] * kv_heads + head_pick
    outgoing = kv_pool.reshape(pool_dev * kv_heads, block_len, pair_width)[row_index]
    received = lax.all_to_all(outgoing, ("grp", "tp"), split_axis=0, concat_axis=0, tiled=True)
    my_table = lax.dynamic_slice_in_dim(old_table, group_index * seats_group, seats_group, 0)
    source_owner = my_table // pool_dev
    source_local = my_table % pool_dev
    arrival = source_owner * group_share + old_rank[source_owner, source_local]
    fetch_rows = arrival[:, None, :] * kvh_dev + jnp.arange(kvh_dev, dtype=jnp.int32)[None, :, None]
    cached = received.reshape(owners * group_share * kvh_dev, block_len, pair_width)[fetch_rows]
    cached = cached.reshape(seats_group, kvh_dev, key_span, pair_width)
    position = jnp.arange(key_span, dtype=jnp.int32)
    cached = jnp.where(
        position[None, None, :, None] < my_lens[:, None, None, None],
        cached,
        jnp.zeros((), cached.dtype),
    )
    zero_index = jnp.zeros((), jnp.int32)
    grown = jax.vmap(
        lambda cached_seat, fresh_seat, start_at: lax.dynamic_update_slice(
            cached_seat, fresh_seat, (zero_index, start_at, zero_index)
        )
    )(cached, new_kv, my_lens)
    new_content, new_holder, new_rank = slot_layout(
        new_table, owners, pool_dev, seats_group, max_blocks
    )
    owner_ids = jnp.arange(owners, dtype=jnp.int32)
    inverse_pick = (
        jnp.zeros((owners, pool_dev), jnp.int32)
        .at[owner_ids[:, None], new_holder * group_share + new_rank]
        .set(jnp.broadcast_to(jnp.arange(pool_dev, dtype=jnp.int32)[None, :], (owners, pool_dev)))
    )
    local_for = lax.dynamic_slice_in_dim(inverse_pick, group_index * group_share, group_share, 1)
    label_for = new_content[owner_ids[:, None], local_for]
    seat_for = label_for // max_blocks - group_index * seats_group
    block_for = label_for % max_blocks
    store_rows = (
        seat_for[:, :, None] * kvh_dev + jnp.arange(kvh_dev, dtype=jnp.int32)[None, None, :]
    ) * max_blocks + block_for[:, :, None]
    leaving = grown.reshape(seats_group * kvh_dev * max_blocks, block_len, pair_width)[store_rows]
    arrived = lax.all_to_all(leaving, ("grp", "tp"), split_axis=0, concat_axis=0, tiled=True)
    mine_holder = lax.dynamic_index_in_dim(new_holder, my_index, 0, keepdims=False)
    mine_rank = lax.dynamic_index_in_dim(new_rank, my_index, 0, keepdims=False)
    head_ids = jnp.arange(kv_heads, dtype=jnp.int32)
    sender = mine_holder[:, None] * tp_count + (head_ids // kvh_dev)[None, :]
    pool_rows = (sender * group_share + mine_rank[:, None]) * kvh_dev + (head_ids % kvh_dev)[
        None, :
    ]
    new_pool = arrived.reshape(owners * group_share * kvh_dev, block_len, pair_width)[pool_rows]
    group_size = qh_dev // kvh_dev
    row_count = group_size * turn
    query_block = min(512, row_count)
    block_total = row_count // query_block
    turn_index = jnp.arange(row_count, dtype=jnp.int32) % turn
    seat_outputs = []
    for seat_slot in range(seats_group):
        head_outputs = []
        for head_slot in range(kvh_dev):
            key_rows = grown[seat_slot, head_slot, :, :head_dim]
            value_rows = grown[seat_slot, head_slot, :, head_dim:]
            query_rows = queries[
                seat_slot, head_slot * group_size : (head_slot + 1) * group_size
            ].reshape(block_total, query_block, head_dim)
            limits = (my_lens[seat_slot] + turn_index).reshape(block_total, query_block)
            result = lax.map(
                lambda pair_in: attend_block(pair_in[0], pair_in[1], key_rows, value_rows),
                (query_rows, limits),
            )
            head_outputs.append(result.reshape(group_size, turn, head_dim))
        seat_outputs.append(jnp.concatenate(head_outputs, axis=0))
    attention = jnp.stack(seat_outputs, axis=0)
    return (attention, new_pool)


def solution(mesh):
    in_specs = (
        P("grp", "tp", None, None),
        P("grp", "tp", None, None),
        P(("grp", "tp"), None, None, None),
        P(),
        P(),
        P(),
        P(),
    )
    out_specs = (P("grp", "tp", None, None), P(("grp", "tp"), None, None, None))
    return jax.shard_map(local, mesh=mesh, in_specs=in_specs, out_specs=out_specs, check_vma=False)
```

profile of v0, /device:TPU:6, one launch (start us, length us, event | category | flops | bytes accessed | tf_op | source)
XLA Modules:
  0.0 950.6 jit_solution(6321771575941984380)
XLA Ops:
  22.6 15.6 %gather_fusion.3 = bf16[256,128,256]{2,1,0:T(8,128)(2,1)} fusion(bf16[256,128,256]{2,1,0:T(8,128)(2,1)} %bitcast.176, s32[1024]{0:T(1024)S(1)} %pad_clamp_fusion.3), kind=kCustom, calls=%fused_computation.3 | custom fusion | bytes 33555456 | tf_op jit(solution)/shard_map/gather | solution.py:85
  53.9 345.5 %all-to-all-done = bf16[32,4,2,128,256]{4,3,2,1,0:T(8,128)(2,1)} async-done(((bf16[32,4,2,128,256]{4,3,2,1,0:T(8,128)(2,1)}), bf16[32,4,2,128,256]{4,3,2,1,0:T(8,128)(2,1)}, u32[]{:S(2)}, u32[]{:S(2)}) %all-to-all-start) | async-done | bytes 16777248 | tf_op jit(solution)/shard_map/all_to_all | solution.py:86
  399.4 15.6 %gather_fusion.5 = bf16[256,128,256]{2,1,0:T(8,128)(2,1)} fusion(bf16[256,128,256]{2,1,0:T(8,128)(2,1)} %bitcast.19, s32[1024]{0:T(1024)S(1)} %pad_clamp_fusion.2), kind=kCustom, calls=%fused_computation.5 | custom fusion | bytes 33555456 | tf_op jit(solution)/shard_map/gather | solution.py:92
  415.0 14.6 %broadcast_select_fusion = bf16[2,2,8192,256]{3,2,1,0:T(8,128)(2,1)} fusion(bf16[2,2,8192,256]{3,2,1,0:T(8,128)(2,1)} %bitcast.173, pred[2,8192]{1,0:T(4,128)(4,1)S(1)} %iota_compare_fusion.4), kind=kLoop, calls=%fused_computation.70 | loop fusion | flops 8388608 | bytes 33570816 | tf_op jit(solution)/shard_map/jit(_where)/select_n | solution.py:95
  429.6 22.5 %while.45 = (s32[]{:T(128)}, bf16[2,2,8192,256]{3,2,1,0:T(8,128)(2,1)}, s32[2,4]{1,0:T(2,128)S(1)}, bf16[2,2,256,256]{3,2,1,0:T(8,128)(2,1)S(1)}, s32[]{:T(128)}, /*index=5*/s32[4]{0:T(128)S(1)}, s32[]{:T(128)}) while((s32[]{:T(128)}, bf16[2,2,8192,256]{3,2,1,0:T(8,128)(2,1)}, s32[2,4]{1,0:T(2,128)S(1)}, bf16[2,2,256,256]{3,2,1,0:T(8,128)(2,1)S(1)}, ...), condition=%wide.while_cond, body=%wide.while_body.sunk | while | flops 131101 | bytes 1310915 | solution.py:102
  452.1 12.1 %slice_bitcast_fusion.6 = (bf16[8192,128]{1,0:T(8,128)(2,1)}, bf16[8192,128]{1,0:T(8,128)(2,1)}, bf16[8192,128]{1,0:T(8,128)(2,1)}, bf16[8192,128]{1,0:T(8,128)(...) fusion(bf16[2,2,8192,256]{3,2,1,0:T(8,128)(2,1)} %get-tuple-ele, ...), kind=kLoop, calls=%fused_computation.78 | loop fusion | bytes 33554432 | tf_op jit(solution)/shard_map/squeeze | solution.py:142
  464.2 15.5 %gather_fusion.8 = bf16[256,128,256]{2,1,0:T(8,128)(2,1)} fusion(bf16[256,128,256]{2,1,0:T(8,128)(2,1)} %bitcast.172, s32[1024]{0:T(1024)S(1)} %pad_clamp_fusion.1), kind=kCustom, calls=%fused_computation.8 | custom fusion | bytes 33555456 | tf_op jit(solution)/shard_map/gather | solution.py:122
  479.7 21.5 %all-to-all-start.1 = ((bf16[32,4,2,128,256]{4,3,2,1,0:T(8,128)(2,1)}), bf16[32,4,2,128,256]{4,3,2,1,0:T(8,128)(2,1)}, u32[]{:S(2)}, u32[]{:S(2)}) async-start(bf16[32,4,2,128,256]{4,3,2,1,0:T(8,128)(2,1)} %bitcast.174), calls=%async_computation.1 | async-start | bytes 33554432 | tf_op jit(solution)/shard_map/all_to_all | solution.py:123
  501.3 106.5 %while.41 = (s32[]{:T(128)}, bf16[4,512,128]{2,1,0:T(8,128)(2,1)S(1)}, s32[4,512]{1,0:T(4,128)S(1)}, bf16[4,512,128]{2,1,0:T(8,128)(2,1)S(1)}, bf16[8192,128]{1,...) while((s32[]{:T(128)}, bf16[4,512,128]{2,1,0:T(8,128)(2,1)S(1)}, s32[4,512]{1,0:T(4,128)S(1)}, ...), condition=%wide.region_8.9_spmd, body=%wide.region_5.8_spmd.sunk | while | flops 2185296896 | bytes 54804568 | solution.py:147
  501.3 9.5 %fusion.108 = (f32[512]{0:T(512)S(1)}, f32[512,8192]{1,0:T(8,128)}) fusion(bf16[8192,128]{1,0:T(8,128)(2,1)} %get-tuple-element.549, bf16[4,512,128]{2,1,0:T(8,128)(2,1)S(1)} %get-tuple-element.548, s32[]{:T(128)} %get-tuple-element.538, s32[512]{0:T(512)S(1)} %bitcast.185), kind=kOutput, calls=%fused_computation.204.clone.1 | convolution fusion | flops 1090518528 | bytes 19009540 | tf_op jit(solution)/shard_map/while/body/eval_jaxpr/dot_general | solution.py:30
  510.9 8.1 fusion.109
  519.0 9.1 fusion.110
  528.1 9.4 fusion.108
  537.4 8.1 fusion.109
  545.6 9.1 fusion.110
  554.7 9.4 fusion.108
  564.0 8.1 fusion.109
  572.2 9.1 fusion.110
  581.3 9.4 fusion.108
  590.6 8.1 fusion.109
  598.8 9.1 fusion.110
  608.6 105.6 %while.42 = (s32[]{:T(128)}, bf16[4,512,128]{2,1,0:T(8,128)(2,1)S(1)}, s32[4,512]{1,0:T(4,128)S(1)}, bf16[4,512,128]{2,1,0:T(8,128)(2,1)}, bf16[8192,128]{1,0:T(...) while((s32[]{:T(128)}, bf16[4,512,128]{2,1,0:T(8,128)(2,1)S(1)}, s32[4,512]{1,0:T(4,128)S(1)}, ...), condition=%wide.region_12.13_spmd, body=%wide.region_9.12_spmd.sunk | while | flops 2185296896 | bytes 54805076 | solution.py:147
  608.9 10.9 %fusion.113 = (f32[512]{0:T(512)S(1)}, f32[512,8192]{1,0:T(8,128)}) fusion(bf16[8192,128]{1,0:T(8,128)(2,1)} %get-tuple-element.528, bf16[4,512,128]{2,1,0:T(8,128)(2,1)} %get-tuple-element.527, s32[]{:T(128)} %get-tuple-element.517, s32[512]{0:T(512)S(1)} %bitcast.186), kind=kOutput, calls=%fused_computation.205.clone.1 | convolution fusion | flops 1090518528 | bytes 19010048 | tf_op jit(solution)/shard_map/while/body/eval_jaxpr/dot_general | solution.py:30
  619.8 8.1 fusion.114
  635.2 10.9 %fusion.113 = (f32[512]{0:T(512)S(1)}, f32[512,8192]{1,0:T(8,128)}) fusion(bf16[8192,128]{1,0:T(8,128)(2,1)} %get-tuple-element.528, bf16[4,512,128]{2,1,0:T(8,128)(2,1)} %get-tuple-element.527, s32[]{:T(128)} %get-tuple-element.517, s32[512]{0:T(512)S(1)} %bitcast.186), kind=kOutput, calls=%fused_computation.205.clone.1 | convolution fusion | flops 1090518528 | bytes 19010048 | tf_op jit(solution)/shard_map/while/body/eval_jaxpr/dot_general | solution.py:30
  646.2 8.1 fusion.114
  661.6 10.9 %fusion.113 = (f32[512]{0:T(512)S(1)}, f32[512,8192]{1,0:T(8,128)}) fusion(bf16[8192,128]{1,0:T(8,128)(2,1)} %get-tuple-element.528, bf16[4,512,128]{2,1,0:T(8,128)(2,1)} %get-tuple-element.527, s32[]{:T(128)} %get-tuple-element.517, s32[512]{0:T(512)S(1)} %bitcast.186), kind=kOutput, calls=%fused_computation.205.clone.1 | convolution fusion | flops 1090518528 | bytes 19010048 | tf_op jit(solution)/shard_map/while/body/eval_jaxpr/dot_general | solution.py:30
  672.5 8.1 fusion.114
  687.9 10.9 %fusion.113 = (f32[512]{0:T(512)S(1)}, f32[512,8192]{1,0:T(8,128)}) fusion(bf16[8192,128]{1,0:T(8,128)(2,1)} %get-tuple-element.528, bf16[4,512,128]{2,1,0:T(8,128)(2,1)} %get-tuple-element.527, s32[]{:T(128)} %get-tuple-element.517, s32[512]{0:T(512)S(1)} %bitcast.186), kind=kOutput, calls=%fused_computation.205.clone.1 | convolution fusion | flops 1090518528 | bytes 19010048 | tf_op jit(solution)/shard_map/while/body/eval_jaxpr/dot_general | solution.py:30
  698.9 8.1 fusion.114
  716.5 106.5 %while.43 = (s32[]{:T(128)}, bf16[4,512,128]{2,1,0:T(8,128)(2,1)S(1)}, s32[4,512]{1,0:T(4,128)S(1)}, bf16[4,512,128]{2,1,0:T(8,128)(2,1)}, bf16[8192,128]{1,0:T(...) while((s32[]{:T(128)}, bf16[4,512,128]{2,1,0:T(8,128)(2,1)S(1)}, s32[4,512]{1,0:T(4,128)S(1)}, ...), condition=%wide.region_16.17_spmd, body=%wide.region_13.16_spmd.sunk | while | flops 2185296896 | bytes 63193712 | solution.py:147
  717.0 11.1 %fusion.118 = (f32[512]{0:T(512)S(1)}, f32[512,8192]{1,0:T(8,128)}) fusion(bf16[8192,128]{1,0:T(8,128)(2,1)} %get-tuple-element.507, bf16[4,512,128]{2,1,0:T(8,128)(2,1)} %get-tuple-element.506, s32[]{:T(128)} %get-tuple-element.496, s32[512]{0:T(512)S(1)} %bitcast.187), kind=kOutput, calls=%fused_computation.206.clone.1 | convolution fusion | flops 1090518528 | bytes 19010048 | tf_op jit(solution)/shard_map/while/body/eval_jaxpr/dot_general | solution.py:30
  728.0 8.1 fusion.119
  743.5 11.1 %fusion.118 = (f32[512]{0:T(512)S(1)}, f32[512,8192]{1,0:T(8,128)}) fusion(bf16[8192,128]{1,0:T(8,128)(2,1)} %get-tuple-element.507, bf16[4,512,128]{2,1,0:T(8,128)(2,1)} %get-tuple-element.506, s32[]{:T(128)} %get-tuple-element.496, s32[512]{0:T(512)S(1)} %bitcast.187), kind=kOutput, calls=%fused_computation.206.clone.1 | convolution fusion | flops 1090518528 | bytes 19010048 | tf_op jit(solution)/shard_map/while/body/eval_jaxpr/dot_general | solution.py:30
  754.5 8.1 fusion.119
  770.0 11.1 %fusion.118 = (f32[512]{0:T(512)S(1)}, f32[512,8192]{1,0:T(8,128)}) fusion(bf16[8192,128]{1,0:T(8,128)(2,1)} %get-tuple-element.507, bf16[4,512,128]{2,1,0:T(8,128)(2,1)} %get-tuple-element.506, s32[]{:T(128)} %get-tuple-element.496, s32[512]{0:T(512)S(1)} %bitcast.187), kind=kOutput, calls=%fused_computation.206.clone.1 | convolution fusion | flops 1090518528 | bytes 19010048 | tf_op jit(solution)/shard_map/while/body/eval_jaxpr/dot_general | solution.py:30
  781.0 8.1 fusion.119
  796.5 11.1 %fusion.118 = (f32[512]{0:T(512)S(1)}, f32[512,8192]{1,0:T(8,128)}) fusion(bf16[8192,128]{1,0:T(8,128)(2,1)} %get-tuple-element.507, bf16[4,512,128]{2,1,0:T(8,128)(2,1)} %get-tuple-element.506, s32[]{:T(128)} %get-tuple-element.496, s32[512]{0:T(512)S(1)} %bitcast.187), kind=kOutput, calls=%fused_computation.206.clone.1 | convolution fusion | flops 1090518528 | bytes 19010048 | tf_op jit(solution)/shard_map/while/body/eval_jaxpr/dot_general | solution.py:30
  807.6 8.1 fusion.119
  823.9 108.0 %while.44 = (s32[]{:T(128)}, bf16[4,512,128]{2,1,0:T(8,128)(2,1)}, s32[4,512]{1,0:T(4,128)S(1)}, bf16[4,512,128]{2,1,0:T(8,128)(2,1)}, bf16[8192,128]{1,0:T(8,12...) while((s32[]{:T(128)}, bf16[4,512,128]{2,1,0:T(8,128)(2,1)}, s32[4,512]{1,0:T(4,128)S(1)}, ...), condition=%wide.region_20.21_spmd, body=%wide.region_17.20_spmd.sunk | while | flops 2185296896 | bytes 54805584 | solution.py:147
  824.1 11.0 %fusion.123 = (f32[512]{0:T(512)S(1)}, f32[512,8192]{1,0:T(8,128)}) fusion(bf16[8192,128]{1,0:T(8,128)(2,1)} %get-tuple-element.486, bf16[4,512,128]{2,1,0:T(8,128)(2,1)} %get-tuple-element.485, s32[]{:T(128)} %get-tuple-element.475, s32[512]{0:T(512)S(1)} %bitcast.188), kind=kOutput, calls=%fused_computation.207.clone.1 | convolution fusion | flops 1090518528 | bytes 19010048 | tf_op jit(solution)/shard_map/while/body/eval_jaxpr/dot_general | solution.py:30
  835.2 8.1 fusion.124
  851.2 10.9 %fusion.123 = (f32[512]{0:T(512)S(1)}, f32[512,8192]{1,0:T(8,128)}) fusion(bf16[8192,128]{1,0:T(8,128)(2,1)} %get-tuple-element.486, bf16[4,512,128]{2,1,0:T(8,128)(2,1)} %get-tuple-element.485, s32[]{:T(128)} %get-tuple-element.475, s32[512]{0:T(512)S(1)} %bitcast.188), kind=kOutput, calls=%fused_computation.207.clone.1 | convolution fusion | flops 1090518528 | bytes 19010048 | tf_op jit(solution)/shard_map/while/body/eval_jaxpr/dot_general | solution.py:30
  862.1 8.1 fusion.124
  878.1 10.9 %fusion.123 = (f32[512]{0:T(512)S(1)}, f32[512,8192]{1,0:T(8,128)}) fusion(bf16[8192,128]{1,0:T(8,128)(2,1)} %get-tuple-element.486, bf16[4,512,128]{2,1,0:T(8,128)(2,1)} %get-tuple-element.485, s32[]{:T(128)} %get-tuple-element.475, s32[512]{0:T(512)S(1)} %bitcast.188), kind=kOutput, calls=%fused_computation.207.clone.1 | convolution fusion | flops 1090518528 | bytes 19010048 | tf_op jit(solution)/shard_map/while/body/eval_jaxpr/dot_general | solution.py:30
  889.0 8.1 fusion.124
  905.0 10.9 %fusion.123 = (f32[512]{0:T(512)S(1)}, f32[512,8192]{1,0:T(8,128)}) fusion(bf16[8192,128]{1,0:T(8,128)(2,1)} %get-tuple-element.486, bf16[4,512,128]{2,1,0:T(8,128)(2,1)} %get-tuple-element.485, s32[]{:T(128)} %get-tuple-element.475, s32[512]{0:T(512)S(1)} %bitcast.188), kind=kOutput, calls=%fused_computation.207.clone.1 | convolution fusion | flops 1090518528 | bytes 19010048 | tf_op jit(solution)/shard_map/while/body/eval_jaxpr/dot_general | solution.py:30
  934.8 15.6 %gather_fusion.9 = bf16[256,128,256]{2,1,0:T(8,128)(2,1)} fusion(bf16[256,128,256]{2,1,0:T(8,128)(2,1)} %bitcast.45, s32[1024]{0:T(1024)S(1)} %copy-done.11), kind=kCustom, calls=%fused_computation.9 | custom fusion | bytes 33555456 | tf_op jit(solution)/shard_map/gather | solution.py:131
  (168 shorter events, 164.7 us)
Async XLA Ops:
  0.6 1.4 copy-start
  38.2 8.1 copy-start.2
  38.2 8.8 copy-start.14
  38.3 361.2 %all-to-all-start = ((bf16[32,4,2,128,256]{4,3,2,1,0:T(8,128)(2,1)}), bf16[32,4,2,128,256]{4,3,2,1,0:T(8,128)(2,1)}, u32[]{:S(2)}, u32[]{:S(2)}) async-start(bf16[32,4,2,128,256]{4,3,2,1,0:T(8,128)(2,1)} %bitcast.175), calls=%async_computation | async-start | bytes 33554432 | tf_op jit(solution)/shard_map/all_to_all | solution.py:86
  44.7 7.9 copy-start.8
  415.0 14.6 %copy-start.4 = (bf16[2,2,256,256]{3,2,1,0:T(8,128)(2,1)S(1)}, bf16[2,2,256,256]{3,2,1,0:T(8,128)(2,1)}, u32[]{:S(2)}) copy-start(bf16[2,2,256,256]{3,2,1,0:T(8,128)(2,1)} %param.16) | copy-start | bytes 1572868
  415.0 14.6 %copy-start.13 = (s32[4]{0:T(128)S(1)}, s32[4]{0:T(128)}, u32[]{:S(2)}) copy-start(s32[4]{0:T(128)} %constant.503) | copy-start | bytes 52
  479.7 455.0 %all-to-all-start.1 = ((bf16[32,4,2,128,256]{4,3,2,1,0:T(8,128)(2,1)}), bf16[32,4,2,128,256]{4,3,2,1,0:T(8,128)(2,1)}, u32[]{:S(2)}, u32[]{:S(2)}) async-start(bf16[32,4,2,128,256]{4,3,2,1,0:T(8,128)(2,1)} %bitcast.174), calls=%async_computation.1 | async-start | bytes 33554432 | tf_op jit(solution)/shard_map/all_to_all | solution.py:123
  501.3 106.6 %copy-start.7 = (bf16[8192,128]{1,0:T(8,128)(2,1)S(1)}, bf16[8192,128]{1,0:T(8,128)(2,1)}, u32[]{:S(2)}) copy-start(bf16[8192,128]{1,0:T(8,128)(2,1)} %get-tuple-element.515) | copy-start | bytes 6291460
  607.8 0.8 copy-start.9
  607.9 108.5 %copy-start.12 = (s32[4,512]{1,0:T(4,128)S(1)}, s32[4,512]{1,0:T(4,128)}, u32[]{:S(2)}) copy-start(s32[4,512]{1,0:T(4,128)} %broadcast_add_fusion) | copy-start | bytes 24580
  716.4 107.5 %copy-start.5 = (bf16[8192,128]{1,0:T(8,128)(2,1)S(1)}, bf16[8192,128]{1,0:T(8,128)(2,1)}, u32[]{:S(2)}) copy-start(bf16[8192,128]{1,0:T(8,128)(2,1)} %get-tuple-element.473) | copy-start | bytes 6291460
  717.0 19.2 %copy-start.6 = (bf16[8192,128]{1,0:T(8,128)(2,1)S(1)}, bf16[8192,128]{1,0:T(8,128)(2,1)}, u32[]{:S(2)}) copy-start(bf16[8192,128]{1,0:T(8,128)(2,1)} %get-tuple-element.508) | copy-start | bytes 6291460 | tf_op jit(solution)/shard_map/while
  743.5 19.2 %copy-start.6 = (bf16[8192,128]{1,0:T(8,128)(2,1)S(1)}, bf16[8192,128]{1,0:T(8,128)(2,1)}, u32[]{:S(2)}) copy-start(bf16[8192,128]{1,0:T(8,128)(2,1)} %get-tuple-element.508) | copy-start | bytes 6291460 | tf_op jit(solution)/shard_map/while
  770.0 19.2 %copy-start.6 = (bf16[8192,128]{1,0:T(8,128)(2,1)S(1)}, bf16[8192,128]{1,0:T(8,128)(2,1)}, u32[]{:S(2)}) copy-start(bf16[8192,128]{1,0:T(8,128)(2,1)} %get-tuple-element.508) | copy-start | bytes 6291460 | tf_op jit(solution)/shard_map/while
  796.5 19.2 %copy-start.6 = (bf16[8192,128]{1,0:T(8,128)(2,1)S(1)}, bf16[8192,128]{1,0:T(8,128)(2,1)}, u32[]{:S(2)}) copy-start(bf16[8192,128]{1,0:T(8,128)(2,1)} %get-tuple-element.508) | copy-start | bytes 6291460 | tf_op jit(solution)/shard_map/while
  823.0 1.0 copy-start.10
  823.9 109.3 %copy-start.3 = (bf16[1,16,256,128]{3,2,1,0:T(8,128)(2,1)S(1)}, bf16[1,16,256,128]{3,2,1,0:T(8,128)(2,1)}, u32[]{:S(2)}) copy-start(bf16[1,16,256,128]{3,2,1,0:T(8,128)(2,1)} %maximum_bitcast_fusion) | copy-start | bytes 3145732
  823.9 110.8 %copy-start.11 = (s32[1024]{0:T(1024)S(1)}, s32[1024]{0:T(1024)}, u32[]{:S(2)}) copy-start(s32[1024]{0:T(1024)} %pad_clamp_fusion) | copy-start | bytes 12292
  934.8 15.6 %copy-start.1 = (s32[16,64]{1,0:T(8,128)S(1)}, s32[16,64]{1,0:T(8,128)}, u32[]{:S(2)}) copy-start(s32[16,64]{1,0:T(8,128)} %param.21) | copy-start | bytes 12292
where the time goes:
time: 960 us; the launch traced here: 951 us
  waiting for transfers between devices  346 us (36%)
  matrix products  296 us (31%)
  other arithmetic  168 us (18%)
  local copies, waits for them, and re-layouts  111 us (12%)
  starting transfers between devices  28 us (3%)
    all_to_all x1, waiting for transfers between devices, local(): lax.all_to_all(outgoing, ('grp', 'tp'), split_axis=0, concat_axis=0, tile...  346 us
    dot_general x16, matrix products, attend_block(): lax.dot_general(query_rows, key_rows, (((1,), (1,)), ((), ())), preferred...  169 us
    reduce_sum x16, other arithmetic, attend_block(): jnp.sum(weights, axis=1, keepdims=True)  130 us
    dot_general x16, matrix products, attend_block(): jnp.dot(weights, value_rows, preferred_element_type=jnp.float32)  126 us
    all_to_all x1, starting transfers between devices, local(): lax.all_to_all(leaving, ('grp', 'tp'), split_axis=0, concat_axis=0, tiled...  21.5 us
  transfers between devices with their start and end apart: 2, of which 1 were waited for; matrix products, arithmetic and copies ran while one was open for 46% of the time, Pallas kernels for 0%

commit v1 on v0

v1 whole, which is shorter than its diff:
```python
import functools

import jax
import jax.numpy as jnp
from jax import lax
from jax.experimental import pallas as pl
from jax.experimental.pallas import tpu as pltpu
from jax.sharding import PartitionSpec as P

VMEM_LIMIT = 50 * 1024 * 1024


def merge_kernel(lanes, block_len, rows_ref, cut_ref, fresh_ref, *refs):
    cached_refs, fresh, out = refs[:lanes], refs[lanes], refs[lanes + 1]
    step = pl.program_id(0)
    for lane in range(lanes):
        cached = cached_refs[lane]
        cut = cut_ref[step * lanes + lane]
        fill = fresh_ref[step * lanes + lane]

        @pl.when(cut == block_len)
        def _():
            out[lane] = cached[0]

        @pl.when(cut == 0)
        def _():
            out[lane] = fresh[fill]

        @pl.when(jnp.logical_and(cut > 0, cut < block_len))
        def _():
            row = lax.broadcasted_iota(jnp.int32, cached.shape[1:], 0)
            out[lane] = jnp.where(
                row < cut, cached[0].astype(jnp.float32), fresh[fill].astype(jnp.float32)
            ).astype(out.dtype)


def merge(received, fresh, rows, cut, fill):
    total, block_len, width = received.shape
    lanes = 8
    spec = lambda lane: pl.BlockSpec(
        (1, block_len, width), lambda s, rows, cut, fill: (rows[s * lanes + lane], 0, 0)
    )
    return pl.pallas_call(
        functools.partial(merge_kernel, lanes, block_len),
        grid_spec=pltpu.PrefetchScalarGridSpec(
            num_scalar_prefetch=3,
            grid=(total // lanes,),
            in_specs=[spec(lane) for lane in range(lanes)]
            + [pl.BlockSpec(fresh.shape, lambda s, *_: (0, 0, 0))],
            out_specs=pl.BlockSpec((lanes, block_len, width), lambda s, *_: (s, 0, 0)),
        ),
        out_shape=jax.ShapeDtypeStruct(received.shape, received.dtype),
        compiler_params=pltpu.CompilerParams(vmem_limit_bytes=VMEM_LIMIT),
        cost_estimate=pl.CostEstimate(
            flops=0, bytes_accessed=4 * total * block_len * width, transcendentals=0
        ),
        name="merge_blocks",
    )(rows, cut, fill, *([received] * lanes), fresh)


def store_kernel(lanes, heads, rows_ref, *refs):
    ins, out = refs[: lanes * heads], refs[-1]
    for lane in range(lanes):
        for head in range(heads):
            out[lane, head, 0] = ins[lane * heads + head][0]


def store(arrived, rows, pool, pool_shape, head_slot):
    unused_total, block_len, width = arrived.shape
    pool_dev, heads = pool_shape[:2]
    lanes = 2
    spec = lambda lane, head: pl.BlockSpec(
        (1, block_len, width),
        lambda s, rows: (rows[(s * lanes + lane) * heads + head], 0, 0),
    )
    in_specs = [spec(lane, head) for lane in range(lanes) for head in range(heads)]
    operands = [arrived] * (lanes * heads)
    aliases = {}
    if pool is not None:
        in_specs.append(pl.BlockSpec(memory_space=pl.ANY))
        operands.append(pool)
        aliases = {len(operands): 0}
    return pl.pallas_call(
        functools.partial(store_kernel, lanes, heads),
        grid_spec=pltpu.PrefetchScalarGridSpec(
            num_scalar_prefetch=1,
            grid=(pool_dev // lanes,),
            in_specs=in_specs,
            out_specs=pl.BlockSpec(
                (lanes, heads, 1, block_len, width), lambda s, rows: (s, 0, head_slot, 0, 0)
            ),
        ),
        out_shape=jax.ShapeDtypeStruct(pool_shape, arrived.dtype),
        input_output_aliases=aliases,
        compiler_params=pltpu.CompilerParams(vmem_limit_bytes=VMEM_LIMIT),
        cost_estimate=pl.CostEstimate(
            flops=0, bytes_accessed=4 * arrived.size, transcendentals=0
        ),
        name="store_blocks",
    )(rows, *operands)


def attend_kernel(pages, block_len, turn, tile, scale, places_ref, lens_ref, *refs):
    page_refs = refs[:pages]
    query, out, total, high, norm = refs[pages:]
    seat, step = pl.program_id(0), pl.program_id(1)
    head_dim, rows = query.shape[1:]
    span = pages * block_len
    length = lens_ref[seat]
    base = step * span
    factor = scale * 1.4426950408889634

    @pl.when(step == 0)
    def _():
        total[...] = jnp.zeros_like(total)
        norm[...] = jnp.zeros_like(norm)
        high[...] = jnp.full_like(high, -1e30)

    def update(masked):
        keys = jnp.concatenate([page[0, :, :head_dim] for page in page_refs], axis=0)
        values = jnp.concatenate([page[0, :, head_dim:] for page in page_refs], axis=0)
        values_t = values.T
        for at in range(0, rows, tile):
            part = pl.ds(at, tile)
            scores = jnp.dot(keys, query[0, :, part], preferred_element_type=jnp.float32)
            if masked:
                column = lax.broadcasted_iota(jnp.int32, scores.shape, 0) + base
                limit = (lax.broadcasted_iota(jnp.int32, scores.shape, 1) + at) % turn + length
                scores = jnp.where(column <= limit, scores, -1e30)
            before = high[:, part]
            now = jnp.maximum(before, jnp.max(scores, axis=0, keepdims=True))
            weights = jnp.exp2((scores - now) * factor)
            fade = jnp.exp2((before - now) * factor)
            high[:, part] = now
            norm[:, part] = norm[:, part] * fade + jnp.sum(weights, axis=0, keepdims=True)
            total[:, part] = total[:, part] * fade + jnp.dot(
                values_t, weights.astype(jnp.bfloat16), preferred_element_type=jnp.float32
            )

    @pl.when(base + span - 1 <= length)
    def _():
        update(False)

    @pl.when(jnp.logical_and(base + span - 1 > length, base < length + turn))
    def _():
        update(True)

    @pl.when(step == pl.num_programs(1) - 1)
    def _():
        out[0] = (total[...] / norm[...]).astype(out.dtype)


def attend(grown, query_t, places, lens, turn, max_blocks):
    seats, head_dim, rows = query_t.shape
    unused_total, block_len, width = grown.shape
    pages = 4
    span = pages * block_len
    steps = max_blocks // pages

    def spec(page):
        def index(seat, step, places, lens):
            last = (lens[seat] + turn - 1) // span
            return (places[seat * max_blocks + jnp.minimum(step, last) * pages + page], 0, 0)

        return pl.BlockSpec((1, block_len, width), index)

    by_seat = pl.BlockSpec((1, head_dim, rows), lambda seat, step, *_: (seat, 0, 0))
    work = seats * rows * max_blocks * block_len
    return pl.pallas_call(
        functools.partial(
            attend_kernel, pages, block_len, turn, min(512, rows), head_dim ** (-0.5)
        ),
        grid_spec=pltpu.PrefetchScalarGridSpec(
            num_scalar_prefetch=2,
            grid=(seats, steps),
            in_specs=[spec(page) for page in range(pages)] + [by_seat],
            out_specs=by_seat,
            scratch_shapes=[
                pltpu.VMEM((head_dim, rows), jnp.float32),
                pltpu.VMEM((1, rows), jnp.float32),
                pltpu.VMEM((1, rows), jnp.float32),
            ],
        ),
        out_shape=jax.ShapeDtypeStruct(query_t.shape, query_t.dtype),
        compiler_params=pltpu.CompilerParams(vmem_limit_bytes=VMEM_LIMIT),
        cost_estimate=pl.CostEstimate(
            flops=4 * work * head_dim, bytes_accessed=2 * grown.size, transcendentals=work
        ),
        name="attend_head",
    )(places, lens, *([grown] * pages), query_t)


def pool_places(slots, session_group, my_index, pool_dev, share):
    mine = my_index * pool_dev + jnp.arange(pool_dev, dtype=jnp.int32)
    match = slots[None] == mine[:, None, None]
    group = jnp.sum(jnp.where(match, session_group[None, :, None], 0), axis=(1, 2))
    local = jnp.arange(pool_dev, dtype=jnp.int32)
    earlier = jnp.logical_and(group[None, :] == group[:, None], local[None, :] < local[:, None])
    return group, jnp.sum(earlier.astype(jnp.int32), axis=1)


def group_places(table, pool_dev, share):
    slots = table.reshape(-1)
    owner = slots // pool_dev
    earlier = jnp.logical_and(owner[None, :] == owner[:, None], slots[None, :] < slots[:, None])
    return owner * share + jnp.sum(earlier.astype(jnp.int32), axis=1)


def local(queries, new_kv, kv_pool, cache_lens, session_seat, old_slots, new_slots):
    group_count = lax.axis_size("grp")
    tp_count = lax.axis_size("tp")
    owners = group_count * tp_count
    pool_dev, kv_heads, block_len, width = kv_pool.shape
    head_dim = width // 2
    seats, qh_dev, turn, unused_dim = queries.shape
    kvh_dev = new_kv.shape[1]
    group_size = qh_dev // kvh_dev
    max_blocks = old_slots.shape[1]
    share = pool_dev // group_count
    group_index = lax.axis_index("grp")
    my_index = group_index * tp_count + lax.axis_index("tp")
    session_group = session_seat // seats

    group, rank = pool_places(old_slots, session_group, my_index, pool_dev, share)
    locals_ = jnp.arange(pool_dev, dtype=jnp.int32)
    order = jnp.sum(
        jnp.where((group * share + rank)[None, :] == locals_[:, None], locals_[None, :], 0), axis=1
    )
    pick = jnp.repeat(order.reshape(group_count, 1, share), tp_count, axis=1)
    head = jnp.arange(tp_count, dtype=jnp.int32)[None, :, None] * kvh_dev
    first_row = (pick * kv_heads + head).reshape(owners, share)
    pool_rows = kv_pool.reshape(pool_dev * kv_heads, block_len, width)

    seat_ids = group_index * seats + jnp.arange(seats, dtype=jnp.int32)
    here = session_seat[None, :] == seat_ids[:, None]
    lens = jnp.sum(jnp.where(here, cache_lens[None, :], 0), axis=1)
    old_table = jnp.sum(jnp.where(here[:, :, None], old_slots[None], 0), axis=1)
    new_table = jnp.sum(jnp.where(here[:, :, None], new_slots[None], 0), axis=1)
    arrival = group_places(old_table, pool_dev, share)
    leave = group_places(new_table, pool_dev, share)
    block = jnp.arange(max_blocks, dtype=jnp.int32)[None, :]
    fresh_blocks = turn // block_len + 2
    cut = jnp.clip(lens[:, None] - block * block_len, 0, block_len)
    beyond = block - lens[:, None] // block_len
    beyond = jnp.where(
        jnp.logical_and(beyond >= 0, beyond < fresh_blocks - 1), beyond, fresh_blocks - 1
    )
    fill = beyond + fresh_blocks * jnp.arange(seats, dtype=jnp.int32)[:, None]
    at = leave[None, :] == jnp.arange(seats * max_blocks, dtype=jnp.int32)[:, None]
    by_leave = lambda per_block: jnp.sum(jnp.where(at, per_block.reshape(1, -1), 0), axis=1)
    merge_rows, merge_cut, merge_fill = by_leave(arrival), by_leave(cut), by_leave(fill)

    blank = jnp.zeros((kvh_dev, fresh_blocks * block_len, width), new_kv.dtype)
    fresh = jnp.stack(
        [
            lax.dynamic_update_slice(blank, new_kv[seat], (0, lens[seat] % block_len, 0))
            for seat in range(seats)
        ]
    ).reshape(seats, kvh_dev, fresh_blocks, block_len, width)

    new_group, new_rank = pool_places(new_slots, session_group, my_index, pool_dev, share)
    sender = new_group[:, None] * tp_count + jnp.arange(tp_count, dtype=jnp.int32)[None, :]
    store_rows = (sender * share + new_rank[:, None]).reshape(-1)

    query_t = jnp.swapaxes(
        queries.reshape(seats, kvh_dev, group_size * turn, head_dim), 2, 3
    )
    received = [
        lax.all_to_all(
            pool_rows[first_row + slot], ("grp", "tp"), split_axis=0, concat_axis=0, tiled=True
        )
        for slot in range(kvh_dev)
    ]
    grown, arrived, outputs = [], [], []
    for slot in range(kvh_dev):
        grown.append(
            merge(
                received[slot].reshape(owners * share, block_len, width),
                fresh[:, slot].reshape(seats * fresh_blocks, block_len, width),
                merge_rows,
                merge_cut,
                merge_fill,
            )
        )
        arrived.append(
            lax.all_to_all(
                grown[slot].reshape(owners, share, block_len, width),
                ("grp", "tp"),
                split_axis=0,
                concat_axis=0,
                tiled=True,
            )
        )
    for slot in range(kvh_dev):
        result = attend(grown[slot], query_t[:, slot], leave, lens, turn, max_blocks)
        outputs.append(jnp.swapaxes(result, 1, 2).reshape(seats, group_size, turn, head_dim))
    attention = jnp.concatenate(outputs, axis=1)
    pool = None
    pool_shape = (pool_dev, tp_count, kvh_dev, block_len, width)
    for slot in range(kvh_dev):
        blocks = arrived[slot].reshape(owners * share, block_len, width)
        pool = store(blocks, store_rows, pool, pool_shape, slot)
    return (attention, pool.reshape(kv_pool.shape))


def solution(mesh):
    in_specs = (
        P("grp", "tp", None, None),
        P("grp", "tp", None, None),
        P(("grp", "tp"), None, None, None),
        P(),
        P(),
        P(),
        P(),
    )
    out_specs = (P("grp", "tp", None, None), P(("grp", "tp"), None, None, None))
    return jax.shard_map(local, mesh=mesh, in_specs=in_specs, out_specs=out_specs, check_vma=False)
```

time: 960 us -> 795 us (0.83)
  matrix products: 296 us -> 0 us
  Pallas kernels: 0 us -> 181 us
  waiting for transfers between devices: 346 us -> 516 us
  other arithmetic: 168 us -> 5.79 us
  local copies, waits for them, and re-layouts: 111 us -> 35.5 us
  starting transfers between devices: 28 us -> 40.9 us
    dot_general x32 -> x0, matrix products: 296 us -> none  [the longest x16 169 us: attend_block(): lax.dot_general(query_rows, key_rows, (((1,), (1,)), ((), ())), preferred...]
    pallas_call x0 -> x6, Pallas kernels: none -> 181 us  [the longest x2 131 us: attend(): pl.pallas_call(functools.partial(attend_kernel, pages, block_len, turn, m...]
    all_to_all x2 -> x4, waiting for transfers between devices: 346 us -> 516 us  [the longest x2 321 us: local(): lax.all_to_all(pool_rows[first_row + slot], ('grp', 'tp'), split_axis=0,...]
    reduce_sum x17 -> x8, other arithmetic: 131 us -> 3.19 us  [the longest x1 2.11 us: pool_places(): jnp.sum(jnp.where(match, session_group[None, :, None], 0), axis=(1, 2))]
    gather x12 -> x2, local copies, waits for them, and re-layouts: 68.8 us -> 24.9 us  [local(): pool_rows[first_row + slot]]
    scatter x11 -> x0, local copies, waits for them, and re-layouts: 20 us -> none
    select_n x15 -> x5, other arithmetic: 15.6 us -> 0.71 us  [the longest x1 0.67 us: local(): session_group = session_seat // seats]
    all_to_all x2 -> x4, starting transfers between devices: 28 us -> 40.9 us  [the longest x2 23.2 us: local(): lax.all_to_all(grown[slot].reshape(owners, share, block_len, width), ('gr...]
  transfers between devices with their start and end apart: 2 -> 4, of which waited for: 1 -> 4; matrix products, arithmetic and copies ran while one was open for 46% -> 3% of each run, Pallas kernels for 0% -> 22%
where the time goes in v1:
time: 795 us; the launch traced here: 783 us
  waiting for transfers between devices  516 us (65%)
  Pallas kernels  181 us (23%)
  starting transfers between devices  40.9 us (5%)
  local copies, waits for them, and re-layouts  35.5 us (4%)
    all_to_all x2, waiting for transfers between devices, local(): lax.all_to_all(pool_rows[first_row + slot], ('grp', 'tp'), split_axis=0,...  321 us
    all_to_all x2, waiting for transfers between devices, local(): lax.all_to_all(grown[slot].reshape(owners, share, block_len, width), ('gr...  195 us
    pallas_call x2, Pallas kernels, attend(): pl.pallas_call(functools.partial(attend_kernel, pages, block_len, turn, m...  131 us
    pallas_call x2, Pallas kernels, merge(): pl.pallas_call(functools.partial(merge_kernel, lanes, block_len), grid_sp...  26 us
    gather x2, local copies, waits for them, and re-layouts, local(): pool_rows[first_row + slot]  24.9 us
    pallas_call x2, Pallas kernels, store(): pl.pallas_call(functools.partial(store_kernel, lanes, heads), grid_spec=p...  24.2 us
    all_to_all x2, starting transfers between devices, local(): lax.all_to_all(grown[slot].reshape(owners, share, block_len, width), ('gr...  23.2 us
    all_to_all x2, starting transfers between devices, local(): lax.all_to_all(pool_rows[first_row + slot], ('grp', 'tp'), split_axis=0,...  17.7 us
  transfers between devices with their start and end apart: 4, of which 4 were waited for; matrix products, arithmetic and copies ran while one was open for 3% of the time, Pallas kernels for 22%

profile of v1, /device:TPU:6, one launch (start us, length us, event | category | flops | bytes accessed | tf_op | source)
XLA Modules:
  0.0 783.4 jit_solution(8246239399037880695)
XLA Ops:
  0.7 0.7 and_select_fusion
  1.3 2.1 select_reduce_fusion
  3.4 0.2 convert_reduce_fusion.2
  3.6 0.1 select_reduce_fusion.5
  3.8 0.1 copy.27
  3.9 0.1 add.200
  4.1 0.1 mul.114
  4.2 0.1 copy.28
  4.3 0.1 reshape.468
  4.4 12.3 %gather_fusion = bf16[128,128,256]{2,1,0:T(8,128)(2,1)} fusion(bf16[256,128,256]{2,1,0:T(8,128)(2,1)} %bitcast.45, s32[1024]{0:T(1024)S(1)} %pad_clamp_fusion.1), kind=kCustom, calls=%fused_computation | custom fusion | bytes 16777728 | tf_op jit(solution)/shard_map/gather | solution.py:270
  16.8 6.1 all-to-all-start
  22.9 0.1 copy.33
  23.0 0.1 reshape.476
  23.1 12.5 %gather_fusion.1 = bf16[128,128,256]{2,1,0:T(8,128)(2,1)} fusion(bf16[256,128,256]{2,1,0:T(8,128)(2,1)} %bitcast.46, s32[1024]{0:T(1024)S(1)} %pad_clamp_fusion), kind=kCustom, calls=%fused_computation.1 | custom fusion | bytes 16777728 | tf_op jit(solution)/shard_map/gather | solution.py:270
  35.6 165.7 %all-to-all-done = bf16[32,4,128,256]{3,2,1,0:T(8,128)(2,1)} async-done(((bf16[32,4,128,256]{3,2,1,0:T(8,128)(2,1)}), bf16[32,4,128,256]{3,2,1,0:T(8,128)(2,1)}, u32[]{:S(2)}, u32[]{:S(2)}) %all-to-all-start) | async-done | bytes 8388640 | tf_op jit(solution)/shard_map/all_to_all | solution.py:269
  201.3 11.6 %all-to-all-start.1 = ((bf16[32,4,128,256]{3,2,1,0:T(8,128)(2,1)}), bf16[32,4,128,256]{3,2,1,0:T(8,128)(2,1)}, u32[]{:S(2)}, u32[]{:S(2)}) async-start(bf16[32,4,128,256]{3,2,1,0:T(8,128)(2,1)} %bitcast.43), calls=%async_computation.1 | async-start | bytes 16777216 | tf_op jit(solution)/shard_map/all_to_all | solution.py:269
  212.9 0.2 select_reduce_fusion.8
  213.1 0.6 fusion.5
  217.5 0.1 add.193
  217.6 0.1 sub.65
  217.8 0.1 min.12
  217.9 0.1 select_reduce_fusion.6
  218.0 0.1 reshape.452
  218.1 0.1 reshape.451
  218.2 2.0 dynamic_update_slice.9
  220.2 2.0 dynamic_update_slice.8
  222.3 0.2 convert_reduce_fusion.1
  222.5 0.2 convert_reduce_fusion
  222.7 0.1 select_reduce_fusion.2
  222.9 0.1 pad_maximum_fusion.1
  223.0 0.1 fusion.3
  223.1 13.0 %merge_blocks.2.refs_0_.refs_1_.refs_2_.refs_3_ = bf16[128,128,256]{2,1,0:T(8,128)(2,1)} custom-call(s32[128]{0:T(128)S(1)} %get-tuple-element.6.rows_ref, s32[128]{0:T(128)S(1)} %get-tuple-element.5.cut_ref, s32[128]{0:T(128)S(1)} %get-tuple-element.4.fresh_ref, ...), custom_call_target="tpu_custom_call" | custom-call | bytes 16777216 | tf_op jit(solution)/shard_map/merge_blocks/pallas_call | solution.py:43
  236.1 155.2 %all-to-all-done.1 = bf16[32,4,128,256]{3,2,1,0:T(8,128)(2,1)} async-done(((bf16[32,4,128,256]{3,2,1,0:T(8,128)(2,1)}), bf16[32,4,128,256]{3,2,1,0:T(8,128)(2,1)}, u32[]{:S(2)}, u32[]{:S(2)}) %all-to-all-start.1) | async-done | bytes 8388640 | tf_op jit(solution)/shard_map/all_to_all | solution.py:269
  391.3 11.6 %all-to-all-start.3 = ((bf16[32,4,128,256]{3,2,1,0:T(8,128)(2,1)}), bf16[32,4,128,256]{3,2,1,0:T(8,128)(2,1)}, u32[]{:S(2)}, u32[]{:S(2)}) async-start(bf16[32,4,128,256]{3,2,1,0:T(8,128)(2,1)} %bitcast.41), calls=%async_computation.3 | async-start | bytes 16777216 | tf_op jit(solution)/shard_map/all_to_all | solution.py:286
  402.9 13.0 %merge_blocks.3.refs_0_.refs_1_.refs_2_.refs_3_ = bf16[128,128,256]{2,1,0:T(8,128)(2,1)} custom-call(s32[128]{0:T(128)S(1)} %get-tuple-element.6.rows_ref, s32[128]{0:T(128)S(1)} %get-tuple-element.5.cut_ref, s32[128]{0:T(128)S(1)} %get-tuple-element.4.fresh_ref, ...), custom_call_target="tpu_custom_call" | custom-call | bytes 16777216 | tf_op jit(solution)/shard_map/merge_blocks/pallas_call | solution.py:43
  415.9 165.4 %all-to-all-done.3 = bf16[32,4,128,256]{3,2,1,0:T(8,128)(2,1)} async-done(((bf16[32,4,128,256]{3,2,1,0:T(8,128)(2,1)}), bf16[32,4,128,256]{3,2,1,0:T(8,128)(2,1)}, u32[]{:S(2)}, u32[]{:S(2)}) %all-to-all-start.3) | async-done | bytes 8388640 | tf_op jit(solution)/shard_map/all_to_all | solution.py:286
  581.3 11.6 %all-to-all-start.2 = ((bf16[32,4,128,256]{3,2,1,0:T(8,128)(2,1)}), bf16[32,4,128,256]{3,2,1,0:T(8,128)(2,1)}, u32[]{:S(2)}, u32[]{:S(2)}) async-start(bf16[32,4,128,256]{3,2,1,0:T(8,128)(2,1)} %bitcast.42), calls=%async_computation.2 | async-start | bytes 16777216 | tf_op jit(solution)/shard_map/all_to_all | solution.py:286
  593.0 0.1 add.217.rows_ref
  593.1 2.9 copy.32
  596.1 0.2 slice_bitcast_fusion.1
  596.3 65.2 %attend_head.3 = bf16[2,128,2048]{2,1,0:T(8,128)(2,1)S(1)} custom-call(s32[128]{0:T(128)S(1)} %multiply_add_fusion.3.places_ref, s32[2]{0:T(128)S(1)} %get-tuple-element.9.lens_ref, bf16[128,128,256]{2,1,0:T(8,128)(2,1)} %merge_blocks.3.refs_0_.refs_1_.refs_2_.refs_3_, bf16[128,128,256]{2,1,0:T(8,128)(2,1)} %merge_blocks.3.refs_0_.refs_1_.refs_2_.refs_3_, ...), custom_call_target="tpu_custom_call" | custom-call | flops 17179869184 | bytes 8388608 | tf_op jit(solution)/shard_map/attend_head/pallas_call | solution.py:169
  661.5 0.7 copy.37
  662.2 65.5 %attend_head.2 = bf16[2,128,2048]{2,1,0:T(8,128)(2,1)S(1)} custom-call(s32[128]{0:T(128)S(1)} %multiply_add_fusion.3.places_ref, s32[2]{0:T(128)S(1)} %get-tuple-element.9.lens_ref, bf16[128,128,256]{2,1,0:T(8,128)(2,1)} %merge_blocks.2.refs_0_.refs_1_.refs_2_.refs_3_, bf16[128,128,256]{2,1,0:T(8,128)(2,1)} %merge_blocks.2.refs_0_.refs_1_.refs_2_.refs_3_, ...), custom_call_target="tpu_custom_call" | custom-call | flops 17179869184 | bytes 8388608 | tf_op jit(solution)/shard_map/attend_head/pallas_call | solution.py:169
  727.7 0.7 copy.36
  728.3 1.5 pad_maximum_fusion
  729.8 12.1 %store_blocks.2.refs_8_ = bf16[32,4,2,128,256]{4,3,2,1,0:T(8,128)(2,1)} custom-call(s32[128]{0:T(128)S(1)} %add.217.rows_ref, bf16[128,128,256]{2,1,0:T(8,128)(2,1)} %bitcast.24.refs_0_.refs_1_.refs_2_.refs_3_.refs_4_.refs_5_.refs_6_.refs_7_, bf16[128,128,256]{2,1,0:T(8,128)(2,1)} %bitcast.24.refs_0_.refs_1_.refs_2_.refs_3_.refs_4_.refs_5_.refs_6_.refs_7_, ...), custom_call_target="tpu_custom_call" | custom-call | bytes 16777216 | tf_op jit(solution)/shard_map/store_blocks/pallas_call | solution.py:83
  741.9 29.4 %all-to-all-done.2 = bf16[32,4,128,256]{3,2,1,0:T(8,128)(2,1)} async-done(((bf16[32,4,128,256]{3,2,1,0:T(8,128)(2,1)}), bf16[32,4,128,256]{3,2,1,0:T(8,128)(2,1)}, u32[]{:S(2)}, u32[]{:S(2)}) %all-to-all-start.2) | async-done | bytes 8388640 | tf_op jit(solution)/shard_map/all_to_all | solution.py:286
  771.3 12.1 %store_blocks.3 = bf16[32,4,2,128,256]{4,3,2,1,0:T(8,128)(2,1)} custom-call(s32[128]{0:T(128)S(1)} %add.217.rows_ref, bf16[128,128,256]{2,1,0:T(8,128)(2,1)} %bitcast.22.refs_0_.refs_1_.refs_2_.refs_3_.refs_4_.refs_5_.refs_6_.refs_7_, ...), custom_call_target="tpu_custom_call", output_to_operand_aliasing={{}: (9, {})} | custom-call | bytes 16777216 | tf_op jit(solution)/shard_map/store_blocks/pallas_call | solution.py:83
  (36 shorter events, 0.7 us)
Async XLA Ops:
  16.8 184.5 %all-to-all-start = ((bf16[32,4,128,256]{3,2,1,0:T(8,128)(2,1)}), bf16[32,4,128,256]{3,2,1,0:T(8,128)(2,1)}, u32[]{:S(2)}, u32[]{:S(2)}) async-start(bf16[32,4,128,256]{3,2,1,0:T(8,128)(2,1)} %bitcast.44), calls=%async_computation | async-start | bytes 16777216 | tf_op jit(solution)/shard_map/all_to_all | solution.py:269
  201.3 11.7 %copy-start.3 = (s32[16]{0:T(128)S(1)}, s32[16]{0:T(128)}, u32[]{:S(2)}) copy-start(s32[16]{0:T(128)} %param.10) | copy-start | bytes 196
  201.3 11.7 %copy-start.4 = (s32[16]{0:T(128)S(1)}, s32[16]{0:T(128)}, u32[]{:S(2)}) copy-start(s32[16]{0:T(128)} %param.11) | copy-start | bytes 196
  201.3 16.6 %copy-start.1 = (s32[16,64]{1,0:T(8,128)S(1)}, s32[16,64]{1,0:T(8,128)}, u32[]{:S(2)}) copy-start(s32[16,64]{1,0:T(8,128)} %param.12) | copy-start | bytes 12292
  201.3 16.6 %copy-start.2 = (s32[16,64]{1,0:T(8,128)S(1)}, s32[16,64]{1,0:T(8,128)}, u32[]{:S(2)}) copy-start(s32[16,64]{1,0:T(8,128)} %param.13) | copy-start | bytes 12292
  201.3 16.9 %copy-start = (bf16[2,2,256,256]{3,2,1,0:T(8,128)(2,1)S(1)}, bf16[2,2,256,256]{3,2,1,0:T(8,128)(2,1)}, u32[]{:S(2)}) copy-start(bf16[2,2,256,256]{3,2,1,0:T(8,128)(2,1)} %param.8) | copy-start | bytes 1572868
  201.3 190.0 %all-to-all-start.1 = ((bf16[32,4,128,256]{3,2,1,0:T(8,128)(2,1)}), bf16[32,4,128,256]{3,2,1,0:T(8,128)(2,1)}, u32[]{:S(2)}, u32[]{:S(2)}) async-start(bf16[32,4,128,256]{3,2,1,0:T(8,128)(2,1)} %bitcast.43), calls=%async_computation.1 | async-start | bytes 16777216 | tf_op jit(solution)/shard_map/all_to_all | solution.py:269
  391.3 190.0 %all-to-all-start.3 = ((bf16[32,4,128,256]{3,2,1,0:T(8,128)(2,1)}), bf16[32,4,128,256]{3,2,1,0:T(8,128)(2,1)}, u32[]{:S(2)}, u32[]{:S(2)}) async-start(bf16[32,4,128,256]{3,2,1,0:T(8,128)(2,1)} %bitcast.41), calls=%async_computation.3 | async-start | bytes 16777216 | tf_op jit(solution)/shard_map/all_to_all | solution.py:286
  581.3 190.0 %all-to-all-start.2 = ((bf16[32,4,128,256]{3,2,1,0:T(8,128)(2,1)}), bf16[32,4,128,256]{3,2,1,0:T(8,128)(2,1)}, u32[]{:S(2)}, u32[]{:S(2)}) async-start(bf16[32,4,128,256]{3,2,1,0:T(8,128)(2,1)} %bitcast.42), calls=%async_computation.2 | async-start | bytes 16777216 | tf_op jit(solution)/shard_map/all_to_all | solution.py:286

commit v2 on v1

--- a/solution.py
+++ b/solution.py
@@ -58,37 +58,70 @@
     )(rows, cut, fill, *([received] * lanes), fresh)
 
 
-def store_kernel(lanes, heads, rows_ref, *refs):
-    ins, out = refs[: lanes * heads], refs[-1]
-    for lane in range(lanes):
-        for head in range(heads):
-            out[lane, head, 0] = ins[lane * heads + head][0]
+def take_kernel(count, rows_ref, source, out, done):
+    copies = [
+        pltpu.make_async_copy(source.at[rows_ref[at]], out.at[at], done.at[at])
+        for at in range(count)
+    ]
+    for copy in copies:
+        copy.start()
+    for copy in copies:
+        copy.wait()
+
+
+def take(source, rows):
+    count = rows.shape[0]
+    shape = (count,) + source.shape[1:]
+    return pl.pallas_call(
+        functools.partial(take_kernel, count),
+        grid_spec=pltpu.PrefetchScalarGridSpec(
+            num_scalar_prefetch=1,
+            grid=(1,),
+            in_specs=[pl.BlockSpec(memory_space=pl.ANY)],
+            out_specs=pl.BlockSpec(memory_space=pl.ANY),
+            scratch_shapes=[pltpu.SemaphoreType.DMA((count,))],
+        ),
+        out_shape=jax.ShapeDtypeStruct(shape, source.dtype),
+        compiler_params=pltpu.CompilerParams(vmem_limit_bytes=VMEM_LIMIT),
+        cost_estimate=pl.CostEstimate(
+            flops=0, bytes_accessed=4 * count * source.shape[1] * source.shape[2], transcendentals=0
+        ),
+        name="take_blocks",
+    )(rows, source)
+
+
+def store_kernel(pool_dev, heads, head_slot, rows_ref, arrived, *refs):
+    out, done = refs[-2:]
+    copies = [
+        pltpu.make_async_copy(
+            arrived.at[rows_ref[slot * heads + head]],
+            out.at[slot, head, head_slot],
+            done.at[slot * heads + head],
+        )
+        for slot in range(pool_dev)
+        for head in range(heads)
+    ]
+    for copy in copies:
+        copy.start()
+    for copy in copies:
+        copy.wait()
 
 
 def store(arrived, rows, pool, pool_shape, head_slot):
-    unused_total, block_len, width = arrived.shape
     pool_dev, heads = pool_shape[:2]
-    lanes = 2
-    spec = lambda lane, head: pl.BlockSpec(
-        (1, block_len, width),
-        lambda s, rows: (rows[(s * lanes + lane) * heads + head], 0, 0),
-    )
-    in_specs = [spec(lane, head) for lane in range(lanes) for head in range(heads)]
-    operands = [arrived] * (lanes * heads)
+    operands = [arrived]
     aliases = {}
     if pool is not None:
-        in_specs.append(pl.BlockSpec(memory_space=pl.ANY))
         operands.append(pool)
-        aliases = {len(operands): 0}
+        aliases = {2: 0}
     return pl.pallas_call(
-        functools.partial(store_kernel, lanes, heads),
+        functools.partial(store_kernel, pool_dev, heads, head_slot),
         grid_spec=pltpu.PrefetchScalarGridSpec(
             num_scalar_prefetch=1,
-            grid=(pool_dev // lanes,),
-            in_specs=in_specs,
-            out_specs=pl.BlockSpec(
-                (lanes, heads, 1, block_len, width), lambda s, rows: (s, 0, head_slot, 0, 0)
-            ),
+            grid=(1,),
+            in_specs=[pl.BlockSpec(memory_space=pl.ANY)] * len(operands),
+            out_specs=pl.BlockSpec(memory_space=pl.ANY),
+            scratch_shapes=[pltpu.SemaphoreType.DMA((pool_dev * heads,))],
         ),
         out_shape=jax.ShapeDtypeStruct(pool_shape, arrived.dtype),
         input_output_aliases=aliases,
@@ -267,7 +300,13 @@
     )
     received = [
         lax.all_to_all(
-            pool_rows[first_row + slot], ("grp", "tp"), split_axis=0, concat_axis=0, tiled=True
+            take(pool_rows, (first_row + slot).reshape(-1)).reshape(
+                owners, share, block_len, width
+            ),
+            ("grp", "tp"),
+            split_axis=0,
+            concat_axis=0,
+            tiled=True,
         )
         for slot in range(kvh_dev)
     ]

time: 795 us -> 1570 us (1.97)
  Pallas kernels: 181 us -> 1190 us
  waiting for transfers between devices: 516 us -> 320 us
  local copies, waits for them, and re-layouts: 35.5 us -> 10.8 us
    pallas_call x2 -> x4, Pallas kernels: 24.2 us -> 1030 us  [the longest x2 514 us: take(): pl.pallas_call(functools.partial(take_kernel, count), grid_spec=pltpu.Pre...]
    all_to_all x2, waiting for transfers between devices: 321 us -> 155 us  [local(): lax.all_to_all(take(pool_rows, (first_row + slot).reshape(-1)).reshape(ow...]
    all_to_all x2, waiting for transfers between devices: 195 us -> 165 us  [local(): lax.all_to_all(grown[slot].reshape(owners, share, block_len, width), ('gr...]
    gather x2 -> x0, local copies, waits for them, and re-layouts: 24.9 us -> none  [local(): pool_rows[first_row + slot]]
  transfers between devices with their start and end apart: 4 -> 4, of which waited for: 4 -> 2; matrix products, arithmetic and copies ran while one was open for 3% -> 1% of each run, Pallas kernels for 22% -> 43%
where the time goes in v2:
time: 1570 us
  Pallas kernels  1190 us (76%)
  waiting for transfers between devices  320 us (20%)
  starting transfers between devices  35.2 us (2%)
    pallas_call x2, Pallas kernels, take(): pl.pallas_call(functools.partial(take_kernel, count), grid_spec=pltpu.Pre...  514 us
    pallas_call x2, Pallas kernels, store(): pl.pallas_call(functools.partial(store_kernel, pool_dev, heads, head_slot...  514 us
    all_to_all x2, waiting for transfers between devices, local(): lax.all_to_all(grown[slot].reshape(owners, share, block_len, width), ('gr...  165 us
    all_to_all x2, waiting for transfers between devices, local(): lax.all_to_all(take(pool_rows, (first_row + slot).reshape(-1)).reshape(ow...  155 us
    pallas_call x2, Pallas kernels, attend(): pl.pallas_call(functools.partial(attend_kernel, pages, block_len, turn, m...  139 us
  transfers between devices with their start and end apart: 4, of which 2 were waited for; matrix products, arithmetic and copies ran while one was open for 1% of the time, Pallas kernels for 43%

profile of v2, /device:TPU:6, one launch (start us, length us, event | category | flops | bytes accessed | tf_op | source)
XLA Modules:
  0.0 1570.1 jit_solution(5916422088990173784)
XLA Ops:
  0.7 0.7 and_select_fusion
  1.3 2.1 select_reduce_fusion
  3.4 0.2 convert_reduce_fusion.2
  3.6 0.1 select_reduce_fusion.5
  3.8 0.1 mul.106
  3.8 0.1 add.174
  3.9 0.1 mul.107
  4.1 0.1 add.176
  4.2 0.1 add.166
  4.3 0.1 add.167
  4.4 257.0 %take_blocks.2 = bf16[128,128,256]{2,1,0:T(8,128)(2,1)} custom-call(s32[128]{0:T(128)S(1)} %get-tuple-element.17.rows_ref, bf16[256,128,256]{2,1,0:T(8,128)(2,1)} %bitcast.34), custom_call_target="tpu_custom_call" | custom-call | bytes 16777216 | tf_op jit(solution)/shard_map/take_blocks/pallas_call | solution.py:75
  261.4 6.1 all-to-all-start
  267.6 257.0 %take_blocks.3 = bf16[128,128,256]{2,1,0:T(8,128)(2,1)} custom-call(s32[128]{0:T(128)S(1)} %get-tuple-element.18.rows_ref, bf16[256,128,256]{2,1,0:T(8,128)(2,1)} %bitcast.35), custom_call_target="tpu_custom_call" | custom-call | bytes 16777216 | tf_op jit(solution)/shard_map/take_blocks/pallas_call | solution.py:75
  524.6 5.9 all-to-all-start.1
  530.5 0.2 select_reduce_fusion.8
  530.7 0.6 fusion.6
  535.0 0.1 add.160
  535.1 0.1 iota_subtract_fusion
  535.2 0.1 sub.65
  535.3 0.1 subtract_clamp_fusion
  535.4 0.1 min.12
  535.5 0.1 select_reduce_fusion.6
  535.6 0.1 reshape.377
  535.6 0.1 reshape.376
  535.8 2.3 dynamic_update_slice.9
  538.2 2.0 dynamic_update_slice.8
  540.2 0.2 convert_reduce_fusion.1
  540.4 0.2 convert_reduce_fusion
  540.6 0.1 select_reduce_fusion.2
  540.7 0.1 pad_maximum_fusion.1
  540.8 0.1 fusion.3
  540.9 13.0 merge_blocks.2.refs_0_.refs_1_.refs_2_.refs_3_
  553.9 154.9 %all-to-all-done.1 = bf16[32,4,128,256]{3,2,1,0:T(8,128)(2,1)} async-done(((bf16[32,4,128,256]{3,2,1,0:T(8,128)(2,1)}), bf16[32,4,128,256]{3,2,1,0:T(8,128)(2,1)}, u32[]{:S(2)}, u32[]{:S(2)}) %all-to-all-start.1) | async-done | bytes 8388640 | tf_op jit(solution)/shard_map/all_to_all | solution.py:302
  708.9 11.6 all-to-all-start.3
  720.5 13.0 merge_blocks.3.refs_0_.refs_1_.refs_2_.refs_3_
  733.5 165.4 %all-to-all-done.3 = bf16[32,4,128,256]{3,2,1,0:T(8,128)(2,1)} async-done(((bf16[32,4,128,256]{3,2,1,0:T(8,128)(2,1)}), bf16[32,4,128,256]{3,2,1,0:T(8,128)(2,1)}, u32[]{:S(2)}, u32[]{:S(2)}) %all-to-all-start.3) | async-done | bytes 8388640 | tf_op jit(solution)/shard_map/all_to_all | solution.py:325
  898.9 11.6 all-to-all-start.2
  910.5 0.1 multiply_add_fusion
  910.6 0.1 add.184.rows_ref
  910.7 2.9 copy.24
  913.7 0.2 slice_bitcast_fusion.1
  913.8 69.5 %attend_head.2 = bf16[2,128,2048]{2,1,0:T(8,128)(2,1)S(1)} custom-call(s32[128]{0:T(128)S(1)} %multiply_add_fusion.3.places_ref, s32[2]{0:T(128)S(1)} %get-tuple-element.9.lens_ref, bf16[128,128,256]{2,1,0:T(8,128)(2,1)} %merge_blocks.2.refs_0_.refs_1_.refs_2_.refs_3_, bf16[128,128,256]{2,1,0:T(8,128)(2,1)} %merge_blocks.2.refs_0_.refs_1_.refs_2_.refs_3_, ...), custom_call_target="tpu_custom_call" | custom-call | flops 17179869184 | bytes 8388608 | tf_op jit(solution)/shard_map/attend_head/pallas_call | solution.py:202
  983.4 0.7 copy.27
  984.0 69.8 %attend_head.3 = bf16[2,128,2048]{2,1,0:T(8,128)(2,1)S(1)} custom-call(s32[128]{0:T(128)S(1)} %multiply_add_fusion.3.places_ref, s32[2]{0:T(128)S(1)} %get-tuple-element.9.lens_ref, bf16[128,128,256]{2,1,0:T(8,128)(2,1)} %merge_blocks.3.refs_0_.refs_1_.refs_2_.refs_3_, bf16[128,128,256]{2,1,0:T(8,128)(2,1)} %merge_blocks.3.refs_0_.refs_1_.refs_2_.refs_3_, ...), custom_call_target="tpu_custom_call" | custom-call | flops 17179869184 | bytes 8388608 | tf_op jit(solution)/shard_map/attend_head/pallas_call | solution.py:202
  1053.9 0.7 copy.28
  1054.5 1.5 pad_maximum_fusion
  1056.0 257.0 %store_blocks.2.refs_0_ = bf16[32,4,2,128,256]{4,3,2,1,0:T(8,128)(2,1)} custom-call(s32[128]{0:T(128)S(1)} %add.184.rows_ref, bf16[128,128,256]{2,1,0:T(8,128)(2,1)} %bitcast.24.arrived), custom_call_target="tpu_custom_call" | custom-call | bytes 16777216 | tf_op jit(solution)/shard_map/store_blocks/pallas_call | solution.py:117
  1313.0 257.0 %store_blocks.3 = bf16[32,4,2,128,256]{4,3,2,1,0:T(8,128)(2,1)} custom-call(s32[128]{0:T(128)S(1)} %add.184.rows_ref, bf16[128,128,256]{2,1,0:T(8,128)(2,1)} %bitcast.22.arrived, bf16[32,4,2,128,256]{4,3,2,1,0:T(8,128)(2,1)} %store_blocks.2.refs_0_), custom_call_target="tpu_custom_call", output_to_operand_aliasing={{}: (2, {})} | custom-call | bytes 16777216 | tf_op jit(solution)/shard_map/store_blocks/pallas_call | solution.py:117
  (33 shorter events, 0.4 us)
Async XLA Ops:
  261.4 263.1 %all-to-all-start = ((bf16[32,4,128,256]{3,2,1,0:T(8,128)(2,1)}), bf16[32,4,128,256]{3,2,1,0:T(8,128)(2,1)}, u32[]{:S(2)}, u32[]{:S(2)}) async-start(bf16[32,4,128,256]{3,2,1,0:T(8,128)(2,1)} %bitcast.40), calls=%async_computation | async-start | bytes 16777216 | tf_op jit(solution)/shard_map/all_to_all | solution.py:302
  524.5 6.0 copy-start.3
  524.6 6.0 copy-start.4
  524.6 10.9 copy-start.1
  524.6 10.9 copy-start.2
  524.6 11.2 copy-start
  524.6 184.3 %all-to-all-start.1 = ((bf16[32,4,128,256]{3,2,1,0:T(8,128)(2,1)}), bf16[32,4,128,256]{3,2,1,0:T(8,128)(2,1)}, u32[]{:S(2)}, u32[]{:S(2)}) async-start(bf16[32,4,128,256]{3,2,1,0:T(8,128)(2,1)} %bitcast.39), calls=%async_computation.1 | async-start | bytes 16777216 | tf_op jit(solution)/shard_map/all_to_all | solution.py:302
  708.9 190.0 %all-to-all-start.3 = ((bf16[32,4,128,256]{3,2,1,0:T(8,128)(2,1)}), bf16[32,4,128,256]{3,2,1,0:T(8,128)(2,1)}, u32[]{:S(2)}, u32[]{:S(2)}) async-start(bf16[32,4,128,256]{3,2,1,0:T(8,128)(2,1)} %bitcast.38), calls=%async_computation.3 | async-start | bytes 16777216 | tf_op jit(solution)/shard_map/all_to_all | solution.py:325
  898.9 414.1 %all-to-all-start.2 = ((bf16[32,4,128,256]{3,2,1,0:T(8,128)(2,1)}), bf16[32,4,128,256]{3,2,1,0:T(8,128)(2,1)}, u32[]{:S(2)}, u32[]{:S(2)}) async-start(bf16[32,4,128,256]{3,2,1,0:T(8,128)(2,1)} %bitcast.37), calls=%async_computation.2 | async-start | bytes 16777216 | tf_op jit(solution)/shard_map/all_to_all | solution.py:325

commit v3 on v2

--- a/solution.py
+++ b/solution.py
@@ -58,15 +58,32 @@
     )(rows, cut, fill, *([received] * lanes), fresh)
 
 
-def take_kernel(count, rows_ref, source, out, done):
-    copies = [
-        pltpu.make_async_copy(source.at[rows_ref[at]], out.at[at], done.at[at])
-        for at in range(count)
+def relay(sources, held, targets, arrive, leave):
+    inward = [
+        pltpu.make_async_copy(source, held.at[at], arrive.at[at])
+        for at, source in enumerate(sources)
     ]
-    for copy in copies:
+    outward = [
+        pltpu.make_async_copy(held.at[at], target, leave.at[at])
+        for at, target in enumerate(targets)
+    ]
+    for copy in inward:
         copy.start()
-    for copy in copies:
+    for copy, after in zip(inward, outward):
         copy.wait()
+        after.start()
+    for copy in outward:
+        copy.wait()
+
+
+def take_kernel(count, rows_ref, source, out, held, arrive, leave):
+    relay(
+        [source.at[rows_ref[at]] for at in range(count)],
+        held,
+        [out.at[at] for at in range(count)],
+        arrive,
+        leave,
+    )
 
 
 def take(source, rows):
@@ -79,7 +96,11 @@
             grid=(1,),
             in_specs=[pl.BlockSpec(memory_space=pl.ANY)],
             out_specs=pl.BlockSpec(memory_space=pl.ANY),
-            scratch_shapes=[pltpu.SemaphoreType.DMA((count,))],
+            scratch_shapes=[
+                pltpu.VMEM(shape, source.dtype),
+                pltpu.SemaphoreType.DMA((count,)),
+                pltpu.SemaphoreType.DMA((count,)),
+            ],
         ),
         out_shape=jax.ShapeDtypeStruct(shape, source.dtype),
         compiler_params=pltpu.CompilerParams(vmem_limit_bytes=VMEM_LIMIT),
@@ -91,20 +112,15 @@
 
 
 def store_kernel(pool_dev, heads, head_slot, rows_ref, arrived, *refs):
-    out, done = refs[-2:]
-    copies = [
-        pltpu.make_async_copy(
-            arrived.at[rows_ref[slot * heads + head]],
-            out.at[slot, head, head_slot],
-            done.at[slot * heads + head],
-        )
-        for slot in range(pool_dev)
-        for head in range(heads)
-    ]
-    for copy in copies:
-        copy.start()
-    for copy in copies:
-        copy.wait()
+    out, held, arrive, leave = refs[-4:]
+    places = [(slot, head) for slot in range(pool_dev) for head in range(heads)]
+    relay(
+        [arrived.at[rows_ref[slot * heads + head]] for slot, head in places],
+        held,
+        [out.at[slot, head, head_slot] for slot, head in places],
+        arrive,
+        leave,
+    )
 
 
 def store(arrived, rows, pool, pool_shape, head_slot):
@@ -121,7 +137,11 @@
             grid=(1,),
             in_specs=[pl.BlockSpec(memory_space=pl.ANY)] * len(operands),
             out_specs=pl.BlockSpec(memory_space=pl.ANY),
-            scratch_shapes=[pltpu.SemaphoreType.DMA((pool_dev * heads,))],
+            scratch_shapes=[
+                pltpu.VMEM((pool_dev * heads,) + arrived.shape[1:], arrived.dtype),
+                pltpu.SemaphoreType.DMA((pool_dev * heads,)),
+                pltpu.SemaphoreType.DMA((pool_dev * heads,)),
+            ],
         ),
         out_shape=jax.ShapeDtypeStruct(pool_shape, arrived.dtype),
         input_output_aliases=aliases,

time: 1570 us -> 788 us (0.50)
  Pallas kernels: 1190 us -> 141 us
  waiting for transfers between devices: 320 us -> 574 us
    pallas_call x2, Pallas kernels: 514 us -> 18.4 us  [store(): pl.pallas_call(functools.partial(store_kernel, pool_dev, heads, head_slot...]
    pallas_call x2, Pallas kernels: 514 us -> 18.4 us  [take(): pl.pallas_call(functools.partial(take_kernel, count), grid_spec=pltpu.Pre...]
    all_to_all x2, waiting for transfers between devices: 155 us -> 324 us  [local(): lax.all_to_all(take(pool_rows, (first_row + slot).reshape(-1)).reshape(ow...]
    all_to_all x2, waiting for transfers between devices: 165 us -> 250 us  [local(): lax.all_to_all(grown[slot].reshape(owners, share, block_len, width), ('gr...]
    pallas_call x2, Pallas kernels: 139 us -> 78.3 us  [attend(): pl.pallas_call(functools.partial(attend_kernel, pages, block_len, turn, m...]
  transfers between devices with their start and end apart: 4 -> 4, of which waited for: 2 -> 4; matrix products, arithmetic and copies ran while one was open for 1% -> 2% of each run, Pallas kernels for 43% -> 16%
where the time goes in v3:
time: 788 us; the launch traced here: 778 us
  waiting for transfers between devices  574 us (73%)
  Pallas kernels  141 us (18%)
  starting transfers between devices  40.9 us (5%)
  local copies, waits for them, and re-layouts  10.7 us (1%)
    all_to_all x2, waiting for transfers between devices, local(): lax.all_to_all(take(pool_rows, (first_row + slot).reshape(-1)).reshape(ow...  324 us
    all_to_all x2, waiting for transfers between devices, local(): lax.all_to_all(grown[slot].reshape(owners, share, block_len, width), ('gr...  250 us
    pallas_call x2, Pallas kernels, attend(): pl.pallas_call(functools.partial(attend_kernel, pages, block_len, turn, m...  78.3 us
    pallas_call x2, Pallas kernels, merge(): pl.pallas_call(functools.partial(merge_kernel, lanes, block_len), grid_sp...  26.1 us
    all_to_all x2, starting transfers between devices, local(): lax.all_to_all(grown[slot].reshape(owners, share, block_len, width), ('gr...  23.2 us
    pallas_call x2, Pallas kernels, take(): pl.pallas_call(functools.partial(take_kernel, count), grid_spec=pltpu.Pre...  18.4 us
    pallas_call x2, Pallas kernels, store(): pl.pallas_call(functools.partial(store_kernel, pool_dev, heads, head_slot...  18.4 us
    all_to_all x2, starting transfers between devices, local(): lax.all_to_all(take(pool_rows, (first_row + slot).reshape(-1)).reshape(ow...  17.7 us
  transfers between devices with their start and end apart: 4, of which 4 were waited for; matrix products, arithmetic and copies ran while one was open for 2% of the time, Pallas kernels for 16%

profile of v3, /device:TPU:6, one launch (start us, length us, event | category | flops | bytes accessed | tf_op | source)
XLA Modules:
  0.0 777.6 jit_solution(14642977328404599018)
XLA Ops:
  0.7 0.7 and_select_fusion
  1.3 2.1 select_reduce_fusion
  3.4 0.2 convert_reduce_fusion.2
  3.6 0.1 select_reduce_fusion.5
  3.8 0.1 mul.106
  3.8 0.1 add.174
  3.9 0.1 mul.107
  4.1 0.1 add.176
  4.3 0.1 add.167
  4.4 9.2 %take_blocks.2 = bf16[128,128,256]{2,1,0:T(8,128)(2,1)} custom-call(s32[128]{0:T(128)S(1)} %get-tuple-element.17.rows_ref, bf16[256,128,256]{2,1,0:T(8,128)(2,1)} %bitcast.34), custom_call_target="tpu_custom_call" | custom-call | bytes 16777216 | tf_op jit(solution)/shard_map/take_blocks/pallas_call | solution.py:92
  13.7 6.1 all-to-all-start
  19.8 9.2 %take_blocks.3 = bf16[128,128,256]{2,1,0:T(8,128)(2,1)} custom-call(s32[128]{0:T(128)S(1)} %get-tuple-element.18.rows_ref, bf16[256,128,256]{2,1,0:T(8,128)(2,1)} %bitcast.35), custom_call_target="tpu_custom_call" | custom-call | bytes 16777216 | tf_op jit(solution)/shard_map/take_blocks/pallas_call | solution.py:92
  29.0 169.2 %all-to-all-done = bf16[32,4,128,256]{3,2,1,0:T(8,128)(2,1)} async-done(((bf16[32,4,128,256]{3,2,1,0:T(8,128)(2,1)}), bf16[32,4,128,256]{3,2,1,0:T(8,128)(2,1)}, u32[]{:S(2)}, u32[]{:S(2)}) %all-to-all-start) | async-done | bytes 8388640 | tf_op jit(solution)/shard_map/all_to_all | solution.py:322
  198.2 11.6 %all-to-all-start.1 = ((bf16[32,4,128,256]{3,2,1,0:T(8,128)(2,1)}), bf16[32,4,128,256]{3,2,1,0:T(8,128)(2,1)}, u32[]{:S(2)}, u32[]{:S(2)}) async-start(bf16[32,4,128,256]{3,2,1,0:T(8,128)(2,1)} %bitcast.39), calls=%async_computation.1 | async-start | bytes 16777216 | tf_op jit(solution)/shard_map/all_to_all | solution.py:322
  209.9 0.2 select_reduce_fusion.8
  210.0 0.6 fusion.6
  214.4 0.1 add.160
  214.5 0.1 iota_subtract_fusion
  214.5 0.1 sub.65
  214.6 0.1 subtract_clamp_fusion
  214.7 0.1 min.12
  214.8 0.1 select_reduce_fusion.6
  214.9 0.1 reshape.377
  215.0 0.1 reshape.376
  215.1 2.3 dynamic_update_slice.9
  217.5 2.0 dynamic_update_slice.8
  219.4 0.2 convert_reduce_fusion.1
  219.6 0.2 convert_reduce_fusion
  219.8 0.1 select_reduce_fusion.2
  220.0 0.1 pad_maximum_fusion.1
  220.1 0.1 fusion.3
  220.2 13.1 %merge_blocks.2.refs_0_.refs_1_.refs_2_.refs_3_ = bf16[128,128,256]{2,1,0:T(8,128)(2,1)} custom-call(s32[128]{0:T(128)S(1)} %get-tuple-element.6.rows_ref, s32[128]{0:T(128)S(1)} %get-tuple-element.5.cut_ref, s32[128]{0:T(128)S(1)} %get-tuple-element.4.fresh_ref, ...), custom_call_target="tpu_custom_call" | custom-call | bytes 16777216 | tf_op jit(solution)/shard_map/merge_blocks/pallas_call | solution.py:43
  233.3 155.0 %all-to-all-done.1 = bf16[32,4,128,256]{3,2,1,0:T(8,128)(2,1)} async-done(((bf16[32,4,128,256]{3,2,1,0:T(8,128)(2,1)}), bf16[32,4,128,256]{3,2,1,0:T(8,128)(2,1)}, u32[]{:S(2)}, u32[]{:S(2)}) %all-to-all-start.1) | async-done | bytes 8388640 | tf_op jit(solution)/shard_map/all_to_all | solution.py:322
  388.2 11.6 %all-to-all-start.3 = ((bf16[32,4,128,256]{3,2,1,0:T(8,128)(2,1)}), bf16[32,4,128,256]{3,2,1,0:T(8,128)(2,1)}, u32[]{:S(2)}, u32[]{:S(2)}) async-start(bf16[32,4,128,256]{3,2,1,0:T(8,128)(2,1)} %bitcast.38), calls=%async_computation.3 | async-start | bytes 16777216 | tf_op jit(solution)/shard_map/all_to_all | solution.py:345
  399.8 13.1 %merge_blocks.3.refs_0_.refs_1_.refs_2_.refs_3_ = bf16[128,128,256]{2,1,0:T(8,128)(2,1)} custom-call(s32[128]{0:T(128)S(1)} %get-tuple-element.6.rows_ref, s32[128]{0:T(128)S(1)} %get-tuple-element.5.cut_ref, s32[128]{0:T(128)S(1)} %get-tuple-element.4.fresh_ref, ...), custom_call_target="tpu_custom_call" | custom-call | bytes 16777216 | tf_op jit(solution)/shard_map/merge_blocks/pallas_call | solution.py:43
  412.9 165.3 %all-to-all-done.3 = bf16[32,4,128,256]{3,2,1,0:T(8,128)(2,1)} async-done(((bf16[32,4,128,256]{3,2,1,0:T(8,128)(2,1)}), bf16[32,4,128,256]{3,2,1,0:T(8,128)(2,1)}, u32[]{:S(2)}, u32[]{:S(2)}) %all-to-all-start.3) | async-done | bytes 8388640 | tf_op jit(solution)/shard_map/all_to_all | solution.py:345
  578.2 11.6 %all-to-all-start.2 = ((bf16[32,4,128,256]{3,2,1,0:T(8,128)(2,1)}), bf16[32,4,128,256]{3,2,1,0:T(8,128)(2,1)}, u32[]{:S(2)}, u32[]{:S(2)}) async-start(bf16[32,4,128,256]{3,2,1,0:T(8,128)(2,1)} %bitcast.37), calls=%async_computation.2 | async-start | bytes 16777216 | tf_op jit(solution)/shard_map/all_to_all | solution.py:345
  589.9 0.1 add.184.rows_ref
  590.0 2.9 copy.24
  593.0 0.2 slice_bitcast_fusion.1
  593.2 39.1 %attend_head.2 = bf16[2,128,2048]{2,1,0:T(8,128)(2,1)S(1)} custom-call(s32[128]{0:T(128)S(1)} %multiply_add_fusion.3.places_ref, s32[2]{0:T(128)S(1)} %get-tuple-element.9.lens_ref, bf16[128,128,256]{2,1,0:T(8,128)(2,1)} %merge_blocks.2.refs_0_.refs_1_.refs_2_.refs_3_, bf16[128,128,256]{2,1,0:T(8,128)(2,1)} %merge_blocks.2.refs_0_.refs_1_.refs_2_.refs_3_, ...), custom_call_target="tpu_custom_call" | custom-call | flops 17179869184 | bytes 8388608 | tf_op jit(solution)/shard_map/attend_head/pallas_call | solution.py:222
  632.3 0.7 copy.27
  632.9 39.3 %attend_head.3 = bf16[2,128,2048]{2,1,0:T(8,128)(2,1)S(1)} custom-call(s32[128]{0:T(128)S(1)} %multiply_add_fusion.3.places_ref, s32[2]{0:T(128)S(1)} %get-tuple-element.9.lens_ref, bf16[128,128,256]{2,1,0:T(8,128)(2,1)} %merge_blocks.3.refs_0_.refs_1_.refs_2_.refs_3_, bf16[128,128,256]{2,1,0:T(8,128)(2,1)} %merge_blocks.3.refs_0_.refs_1_.refs_2_.refs_3_, ...), custom_call_target="tpu_custom_call" | custom-call | flops 17179869184 | bytes 8388608 | tf_op jit(solution)/shard_map/attend_head/pallas_call | solution.py:222
  672.2 0.7 copy.28
  672.9 1.5 pad_maximum_fusion
  674.4 9.2 %store_blocks.2.refs_0_ = bf16[32,4,2,128,256]{4,3,2,1,0:T(8,128)(2,1)} custom-call(s32[128]{0:T(128)S(1)} %add.184.rows_ref, bf16[128,128,256]{2,1,0:T(8,128)(2,1)} %bitcast.24.arrived), custom_call_target="tpu_custom_call" | custom-call | bytes 16777216 | tf_op jit(solution)/shard_map/store_blocks/pallas_call | solution.py:133
  683.6 84.7 %all-to-all-done.2 = bf16[32,4,128,256]{3,2,1,0:T(8,128)(2,1)} async-done(((bf16[32,4,128,256]{3,2,1,0:T(8,128)(2,1)}), bf16[32,4,128,256]{3,2,1,0:T(8,128)(2,1)}, u32[]{:S(2)}, u32[]{:S(2)}) %all-to-all-start.2) | async-done | bytes 8388640 | tf_op jit(solution)/shard_map/all_to_all | solution.py:345
  768.2 9.2 %store_blocks.3 = bf16[32,4,2,128,256]{4,3,2,1,0:T(8,128)(2,1)} custom-call(s32[128]{0:T(128)S(1)} %add.184.rows_ref, bf16[128,128,256]{2,1,0:T(8,128)(2,1)} %bitcast.22.arrived, bf16[32,4,2,128,256]{4,3,2,1,0:T(8,128)(2,1)} %store_blocks.2.refs_0_), custom_call_target="tpu_custom_call", output_to_operand_aliasing={{}: (2, {})} | custom-call | bytes 16777216 | tf_op jit(solution)/shard_map/store_blocks/pallas_call | solution.py:133
  (33 shorter events, 0.5 us)
Async XLA Ops:
  13.7 184.5 %all-to-all-start = ((bf16[32,4,128,256]{3,2,1,0:T(8,128)(2,1)}), bf16[32,4,128,256]{3,2,1,0:T(8,128)(2,1)}, u32[]{:S(2)}, u32[]{:S(2)}) async-start(bf16[32,4,128,256]{3,2,1,0:T(8,128)(2,1)} %bitcast.40), calls=%async_computation | async-start | bytes 16777216 | tf_op jit(solution)/shard_map/all_to_all | solution.py:322
  198.2 11.7 %copy-start.3 = (s32[16]{0:T(128)S(1)}, s32[16]{0:T(128)}, u32[]{:S(2)}) copy-start(s32[16]{0:T(128)} %param.10) | copy-start | bytes 196
  198.2 11.7 %copy-start.4 = (s32[16]{0:T(128)S(1)}, s32[16]{0:T(128)}, u32[]{:S(2)}) copy-start(s32[16]{0:T(128)} %param.11) | copy-start | bytes 196
  198.2 16.6 %copy-start.1 = (s32[16,64]{1,0:T(8,128)S(1)}, s32[16,64]{1,0:T(8,128)}, u32[]{:S(2)}) copy-start(s32[16,64]{1,0:T(8,128)} %param.12) | copy-start | bytes 12292
  198.2 16.6 %copy-start.2 = (s32[16,64]{1,0:T(8,128)S(1)}, s32[16,64]{1,0:T(8,128)}, u32[]{:S(2)}) copy-start(s32[16,64]{1,0:T(8,128)} %param.13) | copy-start | bytes 12292
  198.2 16.9 %copy-start = (bf16[2,2,256,256]{3,2,1,0:T(8,128)(2,1)S(1)}, bf16[2,2,256,256]{3,2,1,0:T(8,128)(2,1)}, u32[]{:S(2)}) copy-start(bf16[2,2,256,256]{3,2,1,0:T(8,128)(2,1)} %param.8) | copy-start | bytes 1572868
  198.2 190.0 %all-to-all-start.1 = ((bf16[32,4,128,256]{3,2,1,0:T(8,128)(2,1)}), bf16[32,4,128,256]{3,2,1,0:T(8,128)(2,1)}, u32[]{:S(2)}, u32[]{:S(2)}) async-start(bf16[32,4,128,256]{3,2,1,0:T(8,128)(2,1)} %bitcast.39), calls=%async_computation.1 | async-start | bytes 16777216 | tf_op jit(solution)/shard_map/all_to_all | solution.py:322
  388.2 190.0 %all-to-all-start.3 = ((bf16[32,4,128,256]{3,2,1,0:T(8,128)(2,1)}), bf16[32,4,128,256]{3,2,1,0:T(8,128)(2,1)}, u32[]{:S(2)}, u32[]{:S(2)}) async-start(bf16[32,4,128,256]{3,2,1,0:T(8,128)(2,1)} %bitcast.38), calls=%async_computation.3 | async-start | bytes 16777216 | tf_op jit(solution)/shard_map/all_to_all | solution.py:345
  578.2 190.0 %all-to-all-start.2 = ((bf16[32,4,128,256]{3,2,1,0:T(8,128)(2,1)}), bf16[32,4,128,256]{3,2,1,0:T(8,128)(2,1)}, u32[]{:S(2)}, u32[]{:S(2)}) async-start(bf16[32,4,128,256]{3,2,1,0:T(8,128)(2,1)} %bitcast.37), calls=%async_computation.2 | async-start | bytes 16777216 | tf_op jit(solution)/shard_map/all_to_all | solution.py:345
